TPU v7x, 512 devices: a whole 4x4x16 slice. The times are simulated.
512 devices in a mesh: fsdp: 8 (over y, core), expert: 64 (over z, x).
Axes of the slice: x: 4, y: 4, z: 16, core: 2. Of those that a mesh axis runs over, the one named last changes fastest.
Arguments:
- resid: bfloat16 [64, 64, 4096], P('expert', None, 'fsdp'), may hold values from -200 to 200
- norm_gain: float32 [4096], P('fsdp'), may hold values from 0.1 to 1.9
- lengths: int32 [64], replicated, may hold values from 1 to 64, 3072 in all
- route_ids: int32 [64, 64, 2], P('expert'), may hold values from 0 to 7, all different within a row; in each aligned block of 64 rows (0 to 63, 64 to 127, ..., all dimensions but the last counted through in order) at most 24 rows name the same one
- route_weight: float32 [64, 64, 2], P('expert'), may hold values from 0.2 to 1
- w_gate: bfloat16 [4096, 98304], P('fsdp', 'expert'), may hold values from -0.09375 to 0.09375
- w_up: bfloat16 [4096, 98304], P('fsdp', 'expert'), may hold values from -0.09375 to 0.09375
- w_down: bfloat16 [98304, 4096], P('expert', 'fsdp'), may hold values from -0.0546875 to 0.0546875
Outputs:
- moe_out: bfloat16 [64, 64, 4096], P('expert', None, 'fsdp')
Inputs may be any that keep to these rules, and one draw needn't show every extreme that they name: `route_ids`: each row names 2 different experts; within one prompt no expert is named by more than 24 rows.
All inputs are finite; a program needn't handle non-finite values.
Results may differ from a plain program's by a relative error of at most 0.029.
Values may be sent and summed in bfloat16 or wider, within the bound.
A program may use at most 64 MiB of HBM per device.

v0:
```python
import jax
import jax.numpy as jnp
from jax import lax
from jax.sharding import PartitionSpec as P

D = 4096
EXPERTS = 8
TOP = 2
CAP = 24


def on_device(resid, norm_gain, lengths, route_ids, route_weight, w_gate, w_up, w_down):
    seq_len = resid.shape[1]
    feat_share = resid.shape[2]
    resid_rows = resid[0].astype(jnp.float32)
    local_squares = jnp.sum(resid_rows * resid_rows, axis=-1)
    square = lax.psum(local_squares, "fsdp") / D
    normed = (resid_rows * lax.rsqrt(square[:, None] + 1e-05) * norm_gain).astype(jnp.bfloat16)
    chosen = route_ids[0]
    weights = route_weight[0]
    devices = lax.axis_size("expert")
    group_size = devices // EXPERTS
    prompt_index = lax.axis_index("expert")
    my_expert = prompt_index // group_size
    slot_iota = jnp.arange(CAP, dtype=jnp.int32)
    expert_iota = jnp.arange(EXPERTS, dtype=jnp.int32)
    owner_expert = jnp.arange(devices, dtype=jnp.int32) // group_size
    expert_hits = jnp.any(chosen[None, :, :] == expert_iota[:, None, None], axis=-1).astype(
        jnp.int32
    )
    expert_rank = jnp.cumsum(expert_hits, axis=1) - 1
    all_rows, all_chosen = (
        lax.all_gather(normed[None], "expert", axis=0, tiled=True),
        lax.all_gather(chosen[None], "expert", axis=0, tiled=True),
    )
    hit_rows = jnp.any(all_chosen == my_expert, axis=-1).astype(jnp.int32)
    slot_rank = jnp.cumsum(hit_rows, axis=1) - 1
    select = (
        (hit_rows[:, None, :] == 1) & (slot_rank[:, None, :] == slot_iota[None, :, None])
    ).astype(jnp.bfloat16)
    slot_rows = jnp.einsum(
        "jct,jtd->jcd", select, all_rows, preferred_element_type=jnp.float32
    ).astype(jnp.bfloat16)
    dispatched = slot_rows.reshape(devices * CAP, feat_share)
    gate_part = jnp.dot(dispatched, w_gate, preferred_element_type=jnp.float32)
    up_part = jnp.dot(dispatched, w_up, preferred_element_type=jnp.float32)
    gate_sum, up_sum = (
        lax.psum(gate_part.astype(jnp.bfloat16), "fsdp").astype(jnp.float32),
        lax.psum(up_part.astype(jnp.bfloat16), "fsdp").astype(jnp.float32),
    )
    hidden = (jax.nn.silu(gate_sum) * up_sum).astype(jnp.bfloat16)
    out_part = jnp.dot(hidden, w_down, preferred_element_type=jnp.float32).astype(jnp.bfloat16)
    returned = lax.all_to_all(
        out_part.reshape(devices, CAP, feat_share),
        "expert",
        split_axis=0,
        concat_axis=0,
        tiled=True,
    )
    combined = jnp.zeros((seq_len, feat_share), jnp.float32)
    for pick_index in range(TOP):
        picked = chosen[:, pick_index]
        picked_hot = (picked[:, None] == expert_iota[None, :]).astype(jnp.int32)
        slot_of = jnp.sum(picked_hot * expert_rank.T, axis=1)
        pick_table = (
            (owner_expert[None, :, None] == picked[:, None, None])
            & (slot_iota[None, None, :] == slot_of[:, None, None])
        ).astype(jnp.bfloat16)
        fetched = jnp.einsum(
            "tjc,jcd->td", pick_table, returned, preferred_element_type=jnp.float32
        )
        combined = combined + weights[:, pick_index : pick_index + 1] * fetched
    live_rows = (jnp.arange(seq_len, dtype=jnp.int32) < lengths[prompt_index]).astype(jnp.float32)
    return (live_rows[:, None] * combined).astype(jnp.bfloat16)[None]


def solution(mesh):
    return jax.shard_map(
        on_device,
        mesh=mesh,
        in_specs=(
            P("expert", None, "fsdp"),
            P("fsdp"),
            P(),
            P("expert", None, None),
            P("expert", None, None),
            P("fsdp", "expert"),
            P("fsdp", "expert"),
            P("expert", "fsdp"),
        ),
        out_specs=P("expert", None, "fsdp"),
        check_vma=False,
    )
```

profile of v0, /device:TPU:6, one launch (start us, length us, event | category | flops | bytes accessed | tf_op | source)
XLA Modules:
  0.0 418.8 jit_solution(11018734511165410351)
XLA Ops:
  6.5 0.0 copy-start
  6.5 0.0 all-gather.2.cloned.1.call-start
  6.5 1.1 fusion.48
  7.6 14.9 %psum.21 = f32[64]{0:T(128)S(1)} all-reduce(f32[64]{0:T(128)S(1)} %fusion.48), channel_id=1, replica_groups=mesh['fsdp'=8,'expert'=64] {'fsdp'}, use_global_device_ids=true, to_apply=%region_6.7 | all-reduce | flops 64 | bytes 512 | tf_op jit(solution)/shard_map/psum | solution.py:17
  22.5 1.6 fusion.50
  24.0 0.0 all-gather.2.cloned.1.call-update
  24.1 0.0 all-reduce.3.cloned.1.call-start
  24.1 87.8 %all_gather.6 = s32[64,64,2]{1,2,0:T(2,128)S(1)} all-gather(s32[1,64,2]{1,2,0:T(2,128)} %param.11), channel_id=1, replica_groups=mesh['fsdp'=8,'expert'=64] {'expert'}, dimensions={0}, use_global_device_ids=true | all-gather | bytes 33280 | tf_op jit(solution)/shard_map/all_gather | solution.py:34
  112.0 0.1 compare_reduce_fusion
  112.1 0.2 reduce_window_sum.23
  112.3 58.2 %all-gather.2.cloned.1.call-done = bf16[64,64,512]{2,1,0:T(8,128)(2,1)} async-done(((bf16[1,64,512]{2,1,0:T(8,128)(2,1)}), bf16[64,64,512]{2,1,0:T(8,128)(2,1)}) %all-gather.2.cloned.1.call-update) | async-done | bytes 4194320 | tf_op jit(solution)/shard_map/all_gather | solution.py:33
  170.5 2.9 convolution_convert_fusion.2
  173.4 0.0 copy-done
  173.4 0.0 copy-start.3
  173.4 4.3 %convolution_convert_fusion = bf16[1536,1536]{1,0:T(8,128)(2,1)} fusion(bf16[1536,512]{1,0:T(8,128)(2,1)S(1)} %bitcast.45, bf16[512,1536]{1,0:T(8,128)(2,1)S(1)} %copy-done), kind=kOutput, calls=%fused_computation.7 | convolution fusion | flops 2418278400 | bytes 7864320 | tf_op jit(solution)/shard_map/dot_general | solution.py:46
  177.7 0.0 copy-done.3
  177.7 4.3 %convolution_convert_fusion.1 = bf16[1536,1536]{1,0:T(8,128)(2,1)} fusion(bf16[1536,512]{1,0:T(8,128)(2,1)S(1)} %bitcast.46, bf16[512,1536]{1,0:T(8,128)(2,1)S(1)} %copy-done.3), kind=kOutput, calls=%fused_computation.8 | convolution fusion | flops 2418278400 | bytes 7864320 | tf_op jit(solution)/shard_map/dot_general | solution.py:45
  182.0 0.0 copy-start.4
  182.0 0.0 all-reduce.3.cloned.1.call-update
  182.0 126.4 %all-reduce.3.cloned.1.call-done = (bf16[1536,1536]{1,0:T(8,128)(2,1)}, bf16[1536,1536]{1,0:T(8,128)(2,1)}) async-done(((bf16[1536,1536]{1,0:T(8,128)(2,1)}, bf16[1536,1536]{1,0:T(8,128)(2,1)}), (bf16[1536,1536]{1,0:T(8,128)(2,1)}, bf16[1536,1536]{1,0:T(8,128)(2,1)})) %all-reduce.3.cloned.1.call-update) | async-done | bytes 9437200 | tf_op jit(solution)/shard_map/psum | solution.py:49
  308.4 0.0 copy-done.4
  308.4 8.3 %fusion.7 = bf16[1536,512]{1,0:T(8,128)(2,1)} fusion(bf16[1536,512]{1,0:T(8,128)(2,1)S(1)} %copy-done.4, bf16[1536,1536]{1,0:T(8,128)(2,1)} %get-tuple-element.7, bf16[1536,1536]{1,0:T(8,128)(2,1)} %get-tuple-element.8), kind=kOutput, calls=%fused_computation.10 | convolution fusion | flops 2435579904 | bytes 12582912 | tf_op jit(solution)/shard_map/dot_general | solution.py:52
  316.7 0.0 copy-start.1
  316.7 0.0 copy-start.5
  316.7 0.0 copy-start.2
  316.7 15.8 %all-to-all-start = ((bf16[64,24,512]{2,1,0:T(8,128)(2,1)}), bf16[64,24,512]{2,1,0:T(8,128)(2,1)S(1)}, u32[]{:S(2)}, u32[]{:S(2)}) async-start(bf16[64,24,512]{2,1,0:T(8,128)(2,1)} %bitcast.44), calls=%async_computation | async-start | bytes 3145728 | tf_op jit(solution)/shard_map/all_to_all | solution.py:53
  332.5 0.0 copy-done.1
  332.6 0.2 reduce_window_sum.22
  332.8 0.0 copy-done.5
  332.8 0.6 dynamic_slice.3
  333.4 0.6 compare_convert_fusion
  334.1 0.0 copy-done.2
  334.1 0.1 broadcast_compare_fusion.1
  334.2 75.6 %all-to-all-done = bf16[64,24,512]{2,1,0:T(8,128)(2,1)S(1)} async-done(((bf16[64,24,512]{2,1,0:T(8,128)(2,1)}), bf16[64,24,512]{2,1,0:T(8,128)(2,1)S(1)}, u32[]{:S(2)}, u32[]{:S(2)}) %all-to-all-start) | async-done | bytes 1572896 | tf_op jit(solution)/shard_map/all_to_all | solution.py:53
  409.8 0.7 fusion.29
  410.6 1.4 fusion.35
  (10 shorter events, 0.1 us)
Async XLA Ops:
  6.5 166.8 %copy-start = (bf16[512,1536]{1,0:T(8,128)(2,1)S(1)}, bf16[512,1536]{1,0:T(8,128)(2,1)}, u32[]{:S(2)}) copy-start(bf16[512,1536]{1,0:T(8,128)(2,1)} %param.14) | copy-start | bytes 4718596
  6.5 164.0 %all-gather.2.cloned.1.call-start = ((), (), s32[]{:S(2)}) async-start(), calls=%async_computation.1 | async-start | bytes 4259840 | tf_op jit(solution)/shard_map/all_gather | solution.py:33
  24.1 284.3 %all-reduce.3.cloned.1.call-start = ((), (), s32[]{:S(2)}) async-start(), calls=%async_computation.2 | async-start | bytes 18874368 | tf_op jit(solution)/shard_map/psum | solution.py:49
  173.4 4.3 %copy-start.3 = (bf16[512,1536]{1,0:T(8,128)(2,1)S(1)}, bf16[512,1536]{1,0:T(8,128)(2,1)}, u32[]{:S(2)}) copy-start(bf16[512,1536]{1,0:T(8,128)(2,1)} %param.13) | copy-start | bytes 4718596
  182.0 126.4 %copy-start.4 = (bf16[1536,512]{1,0:T(8,128)(2,1)S(1)}, bf16[1536,512]{1,0:T(8,128)(2,1)}, u32[]{:S(2)}) copy-start(bf16[1536,512]{1,0:T(8,128)(2,1)} %param.15) | copy-start | bytes 4718596
  316.7 15.9 %copy-start.1 = (s32[1,64,2]{1,2,0:T(2,128)S(1)}, s32[1,64,2]{1,2,0:T(2,128)}, u32[]{:S(2)}) copy-start(s32[1,64,2]{1,2,0:T(2,128)} %param.11) | copy-start | bytes 1540
  316.7 16.1 %copy-start.5 = (s32[64]{0:T(128)S(1)}, s32[64]{0:T(128)}, u32[]{:S(2)}) copy-start(s32[64]{0:T(128)} %param.10) | copy-start | bytes 772
  316.7 17.4 %copy-start.2 = (f32[1,64,2]{1,2,0:T(2,128)S(1)}, f32[1,64,2]{1,2,0:T(2,128)}, u32[]{:S(2)}) copy-start(f32[1,64,2]{1,2,0:T(2,128)} %param.12) | copy-start | bytes 1540
  316.7 93.1 %all-to-all-start = ((bf16[64,24,512]{2,1,0:T(8,128)(2,1)}), bf16[64,24,512]{2,1,0:T(8,128)(2,1)S(1)}, u32[]{:S(2)}, u32[]{:S(2)}) async-start(bf16[64,24,512]{2,1,0:T(8,128)(2,1)} %bitcast.44), calls=%async_computation | async-start | bytes 3145728 | tf_op jit(solution)/shard_map/all_to_all | solution.py:53
Sparse Core Ops, SparseCore 0:
  24.2 146.2 all-gather.1
  182.2 126.2 all-reduce.2
where the time goes:
time: 419 us
  waiting for transfers between devices  260 us (62%)
  blocking collectives  103 us (25%)
  matrix products  21.9 us (5%)
  starting transfers between devices  15.9 us (4%)
  between operations  13.5 us (3%)
    psum x1, waiting for transfers between devices, on_device(): lax.psum(up_part.astype(jnp.bfloat16), 'fsdp').astype(jnp.float32)  126 us
    all_gather x1, blocking collectives, on_device(): lax.all_gather(chosen[None], 'expert', axis=0, tiled=True)  87.8 us
    all_to_all x1, waiting for transfers between devices, on_device(): lax.all_to_all(out_part.reshape(devices, CAP, feat_share), 'expert', spli...  75.6 us
    all_gather x1, waiting for transfers between devices, on_device(): lax.all_gather(normed[None], 'expert', axis=0, tiled=True)  58.2 us
    all_to_all x1, starting transfers between devices, on_device(): lax.all_to_all(out_part.reshape(devices, CAP, feat_share), 'expert', spli...  15.8 us
    psum x1, blocking collectives, on_device(): square = lax.psum(local_squares, 'fsdp') / D  14.9 us
  transfers between devices with their start and end apart: 3, of which 3 were waited for; matrix products, arithmetic and copies ran while one was open for 0% of the time, Pallas kernels for 0%

commit v1 on v0

v1 whole, which is shorter than its diff:
```python
import jax
import jax.numpy as jnp
from jax import lax
from jax.experimental import pallas as pl
from jax.experimental.pallas import tpu as pltpu
from jax.sharding import PartitionSpec as P

MESH = pl.DeviceIdType.MESH
D = 4096
EXPERTS = 8
CAP = 24
LEN = 64
FEAT = 512
HALF = 768
BLOCK = 2 * CAP
WIDE = 256
CHUNKS = 8
ROWS = 8 * CAP
OWN = ROWS // 4
ORDER = (0, 2, 6, 3, 5, 4, 1, 7)
F32 = jnp.float32
BF16 = jnp.bfloat16


def order_of(i):
    distance = ORDER[0] + 0 * i
    for k in range(1, CHUNKS):
        distance = distance + (ORDER[k] - ORDER[k - 1]) * ((i + CHUNKS - k) // CHUNKS)
    return distance


def to_blocks(left, right):
    return jnp.concatenate([left.reshape(8, CAP, WIDE), right.reshape(8, CAP, WIDE)], axis=1)


def from_blocks(blocks):
    return blocks[:, :CAP, :].reshape(ROWS, WIDE), blocks[:, CAP:, :].reshape(ROWS, WIDE)


def kernel(lengths, resid, gain, chosen, weight, w_gate, w_up, w_down, out,
           squares, sent, slots, w_in, w_out, part, ra, rb, hid, out_mine, out_sent, out_got,
           xs, xr, ret_sent, ret,
           sq_s, sq_r, w_l, w_s, w_r, a_s, a_r, c_s, c_r, d_s, d_r, e_s, e_r, f_s, f_r, g_s, g_r,
           h_s, h_r, i_s, i_r, j_s, j_r, l_s, l_r):
    f = lax.axis_index("fsdp")
    p = lax.axis_index("expert")
    y, core = f // 2, f % 2
    z, x = p // 4, p % 4
    expert, par = z // 2, z % 2
    member = par * 4 + x
    right, left, opp = (y + 1) % 4, (y + 3) % 4, (y + 2) % 4

    def same_group(j):
        other = (member + j) % 8
        return (f, (2 * expert + other // 4) * 4 + other % 4)

    def along_z(e):
        return (f, (2 * e + par) * 4 + x)

    def at_y(row):
        return (row * 2 + core, p)

    twin = (y * 2 + 1 - core, p)

    def expert_of(i):
        return (expert + CHUNKS - order_of(i)) % CHUNKS

    def source_of(i):
        return (expert + order_of(i)) % CHUNKS

    def remote(src, dst, send, recv, device):
        return pltpu.make_async_remote_copy(
            src_ref=src, dst_ref=dst, send_sem=send, recv_sem=recv, device_id=device, device_id_type=MESH
        )

    def cp_sq(j):
        return remote(squares.at[f], squares.at[f], sq_s.at[j - 1], sq_r.at[j - 1], ((f + j) % 8, p))

    def cp_sq_from(j):
        return remote(squares.at[f], squares.at[(f + 8 - j) % 8], sq_s.at[j - 1], sq_r.at[j - 1], ((f + j) % 8, p))

    mine, others = pl.ds(HALF * core, HALF), pl.ds(HALF * (1 - core), HALF)

    def w_local():
        return (
            pltpu.make_async_copy(w_gate.at[:, mine], w_in.at[core, :, pl.ds(0, HALF)], w_l.at[0]),
            pltpu.make_async_copy(w_up.at[:, mine], w_in.at[core, :, pl.ds(HALF, HALF)], w_l.at[1]),
            pltpu.make_async_copy(w_down.at[mine, :], w_out.at[core], w_l.at[2]),
        )

    def w_remote(side):
        return (
            remote(w_gate.at[:, others], w_in.at[side, :, pl.ds(0, HALF)], w_s.at[0], w_r.at[0], twin),
            remote(w_up.at[:, others], w_in.at[side, :, pl.ds(HALF, HALF)], w_s.at[1], w_r.at[1], twin),
            remote(w_down.at[others, :], w_out.at[side], w_s.at[2], w_r.at[2], twin),
        )

    def cp_a(i):
        e = expert_of(i)
        return remote(sent.at[e], slots.at[i, core, x, par], a_s.at[i], a_r.at[i], along_z(e))

    def cp_c(i, j):
        own = slots.at[i, core, x, par]
        return remote(own, own, c_s.at[i, j - 1], c_r.at[i, j - 1], same_group(j))

    def cp_d(i, side):
        return remote(slots.at[i, core], slots.at[i, side], d_s.at[i], d_r.at[i], twin)

    def cp_e(i):
        return (
            remote(part.at[i, opp, 0], ra.at[i, 0], e_s.at[i, 0], e_r.at[i, 0], at_y(right)),
            remote(part.at[i, opp, 1], ra.at[i, 1], e_s.at[i, 1], e_r.at[i, 1], at_y(left)),
        )

    def cp_f(i):
        return (
            remote(part.at[i, right], rb.at[i, 0], f_s.at[i, 0], f_r.at[i, 0], at_y(right)),
            remote(part.at[i, left], rb.at[i, 1], f_s.at[i, 1], f_r.at[i, 1], at_y(left)),
        )

    def cp_g(i, to_right, to_left):
        return (
            remote(hid.at[i, y], hid.at[i, to_right], g_s.at[i, 0], g_r.at[i, 0], at_y(right)),
            remote(hid.at[i, y], hid.at[i, to_left], g_s.at[i, 1], g_r.at[i, 1], at_y(left)),
        )

    def cp_h(i, to_right, to_left):
        return (
            remote(hid.at[i, left, 0], hid.at[i, to_right, 0], h_s.at[i, 0], h_r.at[i, 0], at_y(right)),
            remote(hid.at[i, right, 1], hid.at[i, to_left, 1], h_s.at[i, 1], h_r.at[i, 1], at_y(left)),
        )

    def cp_i(i):
        return remote(out_sent.at[i], out_got.at[i], i_s.at[i], i_r.at[i], twin)

    def cp_j(i, j):
        other = (member + j) % 8
        return remote(xs.at[i, other % 4, other // 4], xr.at[i, j - 1], j_s.at[i, j - 1], j_r.at[i, j - 1], same_group(j))

    def cp_l(i):
        return remote(ret_sent.at[i], ret.at[expert], l_s.at[i], l_r.at[i], along_z(source_of(i)))

    def cp_l_from(i):
        return remote(ret_sent.at[i], ret.at[expert_of(i)], l_s.at[i], l_r.at[i], along_z(source_of(i)))

    for copy in w_local():
        copy.start()
    barrier = pltpu.get_barrier_semaphore()
    for j in range(1, 8):
        pl.semaphore_signal(barrier, inc=1, device_id=((f + j) % 8, p), device_id_type=MESH)
        pl.semaphore_signal(barrier, inc=1, device_id=same_group(j), device_id_type=MESH)
        pl.semaphore_signal(barrier, inc=1, device_id=along_z((expert + j) % 8), device_id_type=MESH)

    rows = resid[...].astype(F32)
    squared = rows * rows
    squares[f] = squared[:, 0:128] + squared[:, 128:256] + squared[:, 256:384] + squared[:, 384:512]
    pl.semaphore_wait(barrier, 21)
    for j in range(1, 8):
        cp_sq(j).start()
    for copy in w_remote(core):
        copy.start()

    live = lax.broadcasted_iota(jnp.int32, (LEN, 1), 0) < lengths[p]
    first, second = chosen[:, 0:1], chosen[:, 1:2]
    lanes = lax.broadcasted_iota(jnp.int32, (LEN, 128), 1)
    hits = jnp.where(((lanes == first) | (lanes == second)) & live, 1.0, 0.0)
    before = jnp.where(
        lax.broadcasted_iota(jnp.int32, (LEN, LEN), 1) < lax.broadcasted_iota(jnp.int32, (LEN, LEN), 0), 1.0, 0.0
    )
    rank = jnp.dot(before.astype(BF16), hits.astype(BF16), preferred_element_type=F32)
    places = lax.broadcasted_iota(jnp.int32, (LEN, ROWS), 1).astype(F32)

    def table(pick):
        slot = jnp.sum(jnp.where(lanes == pick, rank, 0.0), axis=1, keepdims=True)
        place = jnp.where(live, pick.astype(F32) * CAP + slot, -1.0)
        return jnp.where(places == place, 1.0, 0.0)

    table_first, table_second = table(first), table(second)
    choose = (table_first + table_second).astype(BF16)

    for j in range(1, 8):
        cp_sq_from(j).wait_recv()
    total = squares[0]
    for j in range(1, 8):
        total = total + squares[j]
    mean = jnp.sum(total, axis=1, keepdims=True) / D
    normed = (rows * lax.rsqrt(mean + 1e-05) * gain[...]).astype(BF16)
    packed = lax.dot_general(choose, normed, (((0,), (0,)), ((), ())), preferred_element_type=F32)
    sent[...] = to_blocks(packed[:, :WIDE], packed[:, WIDE:]).astype(BF16)
    for i in range(1, CHUNKS):
        cp_a(i).start()
    slots[0, core, x, par] = sent[expert]

    def step(t, carry):
        def stage(offset, body):
            i = t - offset

            @pl.when((i >= 0) & (i < CHUNKS))
            def _():
                body(i)

        def gate_up(i):
            @pl.when(i == 0)
            def _():
                for copy in w_local()[:2]:
                    copy.wait()
                for copy in w_remote(1 - core)[:2]:
                    copy.wait_recv()

            cp_d(i, 1 - core).wait_recv()
            halves = []
            for side in range(2):
                block = slots[i, side].reshape(8, BLOCK, WIDE).astype(F32)
                halves.extend(from_blocks(block))
            operand = jnp.concatenate(halves, axis=1).astype(BF16)
            for h in range(2):
                for n in range(HALF // WIDE):
                    columns = pl.ds(h * HALF + n * WIDE, WIDE)
                    product = jnp.dot(operand[:, :FEAT], w_in[0, :, columns], preferred_element_type=F32)
                    product += jnp.dot(operand[:, FEAT:], w_in[1, :, columns], preferred_element_type=F32)
                    part[i, :, h, :, pl.ds(n * WIDE, WIDE)] = product.reshape(4, OWN, WIDE).astype(BF16)
            for copy in cp_e(i):
                copy.start()

        def second_hop(i):
            from_left, from_right = cp_e(i)
            from_left.wait_recv()
            part[i, right, 0] = (part[i, right, 0].astype(F32) + ra[i, 0].astype(F32)).astype(BF16)
            to_right, to_left = cp_f(i)
            to_right.start()
            from_right.wait_recv()
            part[i, left, 1] = (part[i, left, 1].astype(F32) + ra[i, 1].astype(F32)).astype(BF16)
            to_left.start()

        def activate(i):
            for copy in cp_f(i):
                copy.wait_recv()
            gate = part[i, y, 0].astype(F32) + rb[i, 0, 0].astype(F32) + rb[i, 1, 0].astype(F32)
            up = part[i, y, 1].astype(F32) + rb[i, 0, 1].astype(F32) + rb[i, 1, 1].astype(F32)
            value = (gate / (1.0 + jnp.exp(-gate)) * up).astype(BF16)
            hid[i, y, 0] = value[:, : HALF // 2]
            hid[i, y, 1] = value[:, HALF // 2 :]
            for copy in cp_g(i, y, y):
                copy.start()

        def pass_on(i):
            from_left, from_right = cp_g(i, left, right)
            to_right, to_left = cp_h(i, left, right)
            from_left.wait_recv()
            to_right.start()
            from_right.wait_recv()
            to_left.start()

        def down(i):
            @pl.when(i == 0)
            def _():
                w_local()[2].wait()
                w_remote(1 - core)[2].wait_recv()

            for copy in cp_h(i, opp, opp):
                copy.wait_recv()
            operand = jnp.concatenate(
                [hid[i, :, 0].reshape(ROWS, HALF // 2), hid[i, :, 1].reshape(ROWS, HALF // 2)], axis=1
            )

            def product(side):
                return to_blocks(
                    jnp.dot(operand, w_out[side, :, pl.ds(0, WIDE)], preferred_element_type=F32),
                    jnp.dot(operand, w_out[side, :, pl.ds(WIDE, WIDE)], preferred_element_type=F32),
                )

            out_sent[i] = product(1 - core).astype(BF16)
            cp_i(i).start()
            out_mine[i] = product(core)

        def over_slices(i):
            cp_i(i).wait_recv()
            both = out_mine[i] + out_got[i].astype(F32)
            out_mine[i] = both
            xs[i] = both.reshape(4, 2, BLOCK, WIDE).astype(BF16)
            for j in range(1, 8):
                cp_j(i, j).start()

        def give_back(i):
            for j in range(1, 8):
                cp_j(i, j).wait_recv()
            total = out_mine[i, x * 2 + par]
            for j in range(1, 8):
                total = total + xr[i, j - 1].astype(F32)
            ret_sent[i] = total.astype(BF16)

            @pl.when(i == 0)
            def _():
                ret[expert] = ret_sent[i]

            @pl.when(i > 0)
            def _():
                cp_l(i).start()

        def to_twin(i):
            for j in range(1, 8):
                other = (member + 8 - j) % 8
                from_other = slots.at[i, core, other % 4, other // 4]
                remote(from_other, from_other, c_s.at[i, j - 1], c_r.at[i, j - 1], same_group(j)).wait_recv()
            cp_d(i, core).start()

        def to_group(i):
            @pl.when(i > 0)
            def _():
                cp_a(i).wait_recv()

            for j in range(1, 8):
                cp_c(i, j).start()

        stage(2, gate_up)
        stage(3, second_hop)
        stage(4, activate)
        stage(5, pass_on)
        stage(6, down)
        stage(7, over_slices)
        stage(8, give_back)
        stage(1, to_twin)
        stage(0, to_group)
        return carry

    lax.fori_loop(0, CHUNKS + 8, step, 0)

    for i in range(1, CHUNKS):
        cp_l_from(i).wait_recv()
    halves = [half.astype(BF16) for half in from_blocks(ret[...].astype(F32))]
    for h in range(2):
        got_first = jnp.dot(table_first.astype(BF16), halves[h], preferred_element_type=F32)
        got_second = jnp.dot(table_second.astype(BF16), halves[h], preferred_element_type=F32)
        mixed = weight[:, 0:1] * got_first + weight[:, 1:2] * got_second
        out[:, pl.ds(h * WIDE, WIDE)] = mixed.astype(BF16)

    for j in range(1, 8):
        cp_sq(j).wait_send()
    for copy in w_remote(core):
        copy.wait_send()

    def finish(i, carry):
        @pl.when(i > 0)
        def _():
            cp_a(i).wait_send()
            cp_l(i).wait_send()

        for j in range(1, 8):
            cp_c(i, j).wait_send()
            cp_j(i, j).wait_send()
        cp_d(i, core).wait_send()
        cp_i(i).wait_send()
        for copy in (*cp_e(i), *cp_f(i), *cp_g(i, y, y), *cp_h(i, left, right)):
            copy.wait_send()
        return carry

    lax.fori_loop(0, CHUNKS, finish, 0)


def on_device(resid, norm_gain, lengths, route_ids, route_weight, w_gate, w_up, w_down):
    vmem = pl.BlockSpec(memory_space=pltpu.VMEM)
    whole = pl.BlockSpec(memory_space=pl.ANY)
    dma = pltpu.SemaphoreType.DMA
    n = CHUNKS
    result = pl.pallas_call(
        kernel,
        out_shape=jax.ShapeDtypeStruct((LEN, FEAT), BF16),
        in_specs=[pl.BlockSpec(memory_space=pltpu.SMEM), vmem, vmem, vmem, vmem, whole, whole, whole],
        out_specs=vmem,
        scratch_shapes=[
            pltpu.VMEM((8, LEN, 128), F32),
            pltpu.VMEM((EXPERTS, BLOCK, WIDE), BF16),
            pltpu.VMEM((n, 2, 4, 2, BLOCK, WIDE), BF16),
            pltpu.VMEM((2, FEAT, 2 * HALF), BF16),
            pltpu.VMEM((2, HALF, FEAT), BF16),
            pltpu.VMEM((n, 4, 2, OWN, HALF), BF16),
            pltpu.VMEM((n, 2, OWN, HALF), BF16),
            pltpu.VMEM((n, 2, 2, OWN, HALF), BF16),
            pltpu.VMEM((n, 4, 2, OWN, HALF // 2), BF16),
            pltpu.VMEM((n, 8, BLOCK, WIDE), F32),
            pltpu.VMEM((n, 8, BLOCK, WIDE), BF16),
            pltpu.VMEM((n, 8, BLOCK, WIDE), BF16),
            pltpu.VMEM((n, 4, 2, BLOCK, WIDE), BF16),
            pltpu.VMEM((n, 7, BLOCK, WIDE), BF16),
            pltpu.VMEM((n, BLOCK, WIDE), BF16),
            pltpu.VMEM((EXPERTS, BLOCK, WIDE), BF16),
            dma((7,)), dma((7,)),
            dma((3,)), dma((3,)), dma((3,)),
            dma((n,)), dma((n,)),
            dma((n, 7)), dma((n, 7)),
            dma((n,)), dma((n,)),
            dma((n, 2)), dma((n, 2)),
            dma((n, 2)), dma((n, 2)),
            dma((n, 2)), dma((n, 2)),
            dma((n, 2)), dma((n, 2)),
            dma((n,)), dma((n,)),
            dma((n, 7)), dma((n, 7)),
            dma((n,)), dma((n,)),
        ],
        compiler_params=pltpu.CompilerParams(
            collective_id=0, has_side_effects=True, vmem_limit_bytes=52 << 20
        ),
        cost_estimate=pl.CostEstimate(flops=8_000_000_000, bytes_accessed=5_000_000, transcendentals=1_000_000),
    )(lengths, resid[0], norm_gain[None], route_ids[0], route_weight[0], w_gate, w_up, w_down)
    return result[None]


def solution(mesh):
    return jax.shard_map(
        on_device,
        mesh=mesh,
        in_specs=(
            P("expert", None, "fsdp"),
            P("fsdp"),
            P(),
            P("expert", None, None),
            P("expert", None, None),
            P("fsdp", "expert"),
            P("fsdp", "expert"),
            P("expert", "fsdp"),
        ),
        out_specs=P("expert", None, "fsdp"),
        check_vma=False,
    )
```

time: 419 us -> 127 us (0.30)
  waiting for transfers between devices: 260 us -> 0 us
  Pallas kernels: 0 us -> 121 us
  blocking collectives: 103 us -> 0 us
  matrix products: 21.9 us -> 0 us
  starting transfers between devices: 15.9 us -> 0 us
  between operations: 13.5 us -> 0.01 us
  local copies, waits for them, and re-layouts: 0.62 us -> 5.75 us
    psum x1 -> x0, waiting for transfers between devices: 126 us -> none  [on_device(): lax.psum(up_part.astype(jnp.bfloat16), 'fsdp').astype(jnp.float32)]
    pallas_call x0 -> x1, Pallas kernels: none -> 121 us  [on_device(): pl.pallas_call(kernel, out_shape=jax.ShapeDtypeStruct((LEN, FEAT), BF16),...]
    all_gather x1 -> x0, blocking collectives: 87.8 us -> none  [on_device(): lax.all_gather(chosen[None], 'expert', axis=0, tiled=True)]
    all_to_all x1 -> x0, waiting for transfers between devices: 75.6 us -> none  [on_device(): lax.all_to_all(out_part.reshape(devices, CAP, feat_share), 'expert', spli...]
    all_gather x1 -> x0, waiting for transfers between devices: 58.2 us -> none  [on_device(): lax.all_gather(normed[None], 'expert', axis=0, tiled=True)]
    dot_general x6 -> x0, matrix products: 21.9 us -> none  [the longest x1 8.26 us: on_device(): jnp.dot(hidden, w_down, preferred_element_type=jnp.float32)]
    all_to_all x1 -> x0, starting transfers between devices: 15.8 us -> none  [on_device(): lax.all_to_all(out_part.reshape(devices, CAP, feat_share), 'expert', spli...]
    psum x1 -> x0, blocking collectives: 14.9 us -> none  [on_device(): square = lax.psum(local_squares, 'fsdp') / D]
  transfers between devices with their start and end apart: 3 -> 0, of which waited for: 3 -> 0; matrix products, arithmetic and copies ran while one was open for 0% -> 0% of each run, Pallas kernels for 0% -> 0%
where the time goes in v1:
time: 127 us
  Pallas kernels  121 us (95%)
  local copies, waits for them, and re-layouts  5.75 us (5%)
    pallas_call x1, Pallas kernels, on_device(): pl.pallas_call(kernel, out_shape=jax.ShapeDtypeStruct((LEN, FEAT), BF16),...  121 us
    unnamed x9, local copies, waits for them, and re-layouts  4.21 us

profile of v1, /device:TPU:6, one launch (start us, length us, event | category | flops | bytes accessed | tf_op | source)
XLA Modules:
  0.0 127.2 jit_solution(17539653076189558645)
XLA Ops:
  0.0 0.8 copy.9.chosen
  0.8 0.8 copy.10.weight
  1.5 0.0 copy-start
  1.5 1.4 %copy-done = bf16[512,1536]{1,0:T(8,128)(2,1)S(1)} copy-done((bf16[512,1536]{1,0:T(8,128)(2,1)S(1)}, bf16[512,1536]{1,0:T(8,128)(2,1)}, u32[]{:S(2)}) %copy-start) | copy-done | bytes 1572888
  2.9 0.0 copy-start.1
  2.9 0.8 copy-done.1
  3.8 0.0 copy-start.2
  3.8 0.7 copy-done.2
  4.5 0.0 copy-start.3
  4.5 0.7 copy-done.3
  5.1 121.4 %shard_map.82 = bf16[64,512]{1,0:T(8,128)(2,1)S(1)} custom-call(s32[64]{0:T(128)S(1)} %copy-done.3, bf16[64,512]{1,0:T(8,128)(2,1)S(1)} %bitcast.6, f32[1,512]{1,0:T(1,128)S(1)} %bitcast.7, s32[64,2]{1,0:T(8,128)S(1)} %copy.9.chosen, f32[64,2]{1,0:T(8,128)S(1)} %copy.10.weight, bf16[512,1536]{1,0:T(8,128)(2,1)S(1)} %copy-done, bf16[512,1536]{1,0:T(8,128)(2,1)} %w_up.1, ...), custom_call_target="tpu_custom_call" | custom-call | flops 8000000000 | bytes 5000000 | tf_op jit(solution)/shard_map/pallas_call | solution.py:365
  126.6 0.6 copy.12
Async XLA Ops:
  1.5 1.4 %copy-start = (bf16[512,1536]{1,0:T(8,128)(2,1)S(1)}, bf16[512,1536]{1,0:T(8,128)(2,1)}, u32[]{:S(2)}) copy-start(bf16[512,1536]{1,0:T(8,128)(2,1)} %w_gate.1) | copy-start | bytes 4718596
  2.9 0.8 copy-start.1
  3.8 0.7 copy-start.2
  4.5 0.7 copy-start.3

commit v2 on v1

--- a/solution.py
+++ b/solution.py
@@ -17,7 +17,7 @@
 CHUNKS = 8
 ROWS = 8 * CAP
 OWN = ROWS // 4
-ORDER = (0, 2, 6, 3, 5, 4, 1, 7)
+ORDER = (0, 1, 2, 6, 3, 5, 4, 7)
 F32 = jnp.float32
 BF16 = jnp.bfloat16
 
@@ -37,8 +37,8 @@
     return blocks[:, :CAP, :].reshape(ROWS, WIDE), blocks[:, CAP:, :].reshape(ROWS, WIDE)
 
 
-def kernel(lengths, resid, gain, chosen, weight, w_gate, w_up, w_down, out,
-           squares, sent, slots, w_in, w_out, part, ra, rb, hid, out_mine, out_sent, out_got,
+def kernel(lengths, resid_in, gain_in, chosen_in, weight_in, w_gate, w_up, w_down, out,
+           resid, gain, gain_s, gain_r, chosen, weight, in_l, sq_sent, sq_got, sent, slots, w_in, w_out, part, ra, rb, hid, out_mine, out_sent, out_got,
            xs, xr, ret_sent, ret,
            sq_s, sq_r, w_l, w_s, w_r, a_s, a_r, c_s, c_r, d_s, d_r, e_s, e_r, f_s, f_r, g_s, g_r,
            h_s, h_r, i_s, i_r, j_s, j_r, l_s, l_r):
@@ -73,11 +73,15 @@
             src_ref=src, dst_ref=dst, send_sem=send, recv_sem=recv, device_id=device, device_id_type=MESH
         )
 
-    def cp_sq(j):
-        return remote(squares.at[f], squares.at[f], sq_s.at[j - 1], sq_r.at[j - 1], ((f + j) % 8, p))
-
-    def cp_sq_from(j):
-        return remote(squares.at[f], squares.at[(f + 8 - j) % 8], sq_s.at[j - 1], sq_r.at[j - 1], ((f + j) % 8, p))
+    def cp_sq(i):
+        return (
+            remote(sq_sent.at[i, right], sq_got.at[i, 0], sq_s.at[i, 0], sq_r.at[i, 0], at_y(right)),
+            remote(sq_sent.at[i, left], sq_got.at[i, 1], sq_s.at[i, 1], sq_r.at[i, 1], at_y(left)),
+            remote(sq_sent.at[i, opp], sq_got.at[i, 2], sq_s.at[i, 2], sq_r.at[i, 2], at_y(opp)),
+        )
+
+    def cp_gain(side):
+        return remote(gain_in, gain.at[side], gain_s, gain_r, twin)
 
     mine, others = pl.ds(HALF * core, HALF), pl.ds(HALF * (1 - core), HALF)
 
@@ -143,65 +147,77 @@
     def cp_l_from(i):
         return remote(ret_sent.at[i], ret.at[expert_of(i)], l_s.at[i], l_r.at[i], along_z(source_of(i)))
 
+    small = [
+        pltpu.make_async_copy(source, target, in_l.at[k])
+        for k, (source, target) in enumerate(
+            ((chosen_in, chosen), (resid_in, resid), (weight_in, weight), (gain_in, gain.at[core]))
+        )
+    ]
+    barrier = pltpu.get_barrier_semaphore()
+    near = [along_z((expert + 1) % 8), along_z((expert + 7) % 8)]
+    near += [same_group(j) for j in range(1, 8)] + [at_y(right), at_y(left), at_y(opp), twin]
+    for device in near:
+        pl.semaphore_signal(barrier, inc=1, device_id=device, device_id_type=MESH)
+    for copy in small:
+        copy.start()
     for copy in w_local():
         copy.start()
-    barrier = pltpu.get_barrier_semaphore()
+
+    def to_column(row, size):
+        shape = (size, 128)
+        diagonal = lax.broadcasted_iota(jnp.int32, shape, 0) == lax.broadcasted_iota(jnp.int32, shape, 1)
+        return jnp.sum(jnp.where(diagonal, row, 0.0), axis=1, keepdims=True)
+
+    small[0].wait()
+    live = lax.broadcasted_iota(jnp.int32, (1, LEN), 1) < lengths[p]
+    first, second = chosen[0:1, :], chosen[1:2, :]
+    experts = lax.broadcasted_iota(jnp.int32, (EXPERTS, LEN), 0)
+    hits = jnp.where(((experts == first) | (experts == second)) & live, 1.0, 0.0)
+    before = jnp.where(
+        lax.broadcasted_iota(jnp.int32, (LEN, LEN), 0) < lax.broadcasted_iota(jnp.int32, (LEN, LEN), 1), 1.0, 0.0
+    )
+    rank = jnp.dot(hits.astype(BF16), before.astype(BF16), preferred_element_type=F32)
+    places = lax.broadcasted_iota(jnp.int32, (ROWS, LEN), 0).astype(F32)
+
+    def table(pick):
+        slot = jnp.sum(jnp.where(experts == pick, rank, 0.0), axis=0, keepdims=True)
+        place = jnp.where(live, pick.astype(F32) * CAP + slot, -1.0)
+        return jnp.where(places == place, 1.0, 0.0)
+
+    table_first, table_second = table(first), table(second)
+    choose = (table_first + table_second).astype(BF16)
+
+    def weight_of(k):
+        row = jnp.concatenate([weight[k : k + 1, :], jnp.zeros((1, 128 - LEN), F32)], axis=1)
+        return to_column(row, LEN)
+
+    small[1].wait()
+    packed = jnp.dot(choose, resid[...], preferred_element_type=F32)
+    sent[...] = to_blocks(packed[:, :WIDE], packed[:, WIDE:]).astype(BF16)
+    slots[0, core, x, par] = sent[expert]
+    pl.semaphore_wait(barrier, len(near))
     for j in range(1, 8):
-        pl.semaphore_signal(barrier, inc=1, device_id=((f + j) % 8, p), device_id_type=MESH)
-        pl.semaphore_signal(barrier, inc=1, device_id=same_group(j), device_id_type=MESH)
-        pl.semaphore_signal(barrier, inc=1, device_id=along_z((expert + j) % 8), device_id_type=MESH)
-
-    rows = resid[...].astype(F32)
-    squared = rows * rows
-    squares[f] = squared[:, 0:128] + squared[:, 128:256] + squared[:, 256:384] + squared[:, 384:512]
-    pl.semaphore_wait(barrier, 21)
-    for j in range(1, 8):
-        cp_sq(j).start()
+        cp_c(0, j).start()
+    cp_a(1).start()
+    cp_a(7).start()
+    cp_gain(core).start()
     for copy in w_remote(core):
         copy.start()
-
-    live = lax.broadcasted_iota(jnp.int32, (LEN, 1), 0) < lengths[p]
-    first, second = chosen[:, 0:1], chosen[:, 1:2]
-    lanes = lax.broadcasted_iota(jnp.int32, (LEN, 128), 1)
-    hits = jnp.where(((lanes == first) | (lanes == second)) & live, 1.0, 0.0)
-    before = jnp.where(
-        lax.broadcasted_iota(jnp.int32, (LEN, LEN), 1) < lax.broadcasted_iota(jnp.int32, (LEN, LEN), 0), 1.0, 0.0
-    )
-    rank = jnp.dot(before.astype(BF16), hits.astype(BF16), preferred_element_type=F32)
-    places = lax.broadcasted_iota(jnp.int32, (LEN, ROWS), 1).astype(F32)
-
-    def table(pick):
-        slot = jnp.sum(jnp.where(lanes == pick, rank, 0.0), axis=1, keepdims=True)
-        place = jnp.where(live, pick.astype(F32) * CAP + slot, -1.0)
-        return jnp.where(places == place, 1.0, 0.0)
-
-    table_first, table_second = table(first), table(second)
-    choose = (table_first + table_second).astype(BF16)
-
-    for j in range(1, 8):
-        cp_sq_from(j).wait_recv()
-    total = squares[0]
-    for j in range(1, 8):
-        total = total + squares[j]
-    mean = jnp.sum(total, axis=1, keepdims=True) / D
-    normed = (rows * lax.rsqrt(mean + 1e-05) * gain[...]).astype(BF16)
-    packed = lax.dot_general(choose, normed, (((0,), (0,)), ((), ())), preferred_element_type=F32)
-    sent[...] = to_blocks(packed[:, :WIDE], packed[:, WIDE:]).astype(BF16)
-    for i in range(1, CHUNKS):
-        cp_a(i).start()
-    slots[0, core, x, par] = sent[expert]
+    for copy in small[2:]:
+        copy.wait()
 
     def step(t, carry):
-        def stage(offset, body):
+        def stage(offset, body, begin=0):
             i = t - offset
 
-            @pl.when((i >= 0) & (i < CHUNKS))
+            @pl.when((i >= begin) & (i < CHUNKS))
             def _():
                 body(i)
 
         def gate_up(i):
             @pl.when(i == 0)
             def _():
+                cp_gain(1 - core).wait_recv()
                 for copy in w_local()[:2]:
                     copy.wait()
                 for copy in w_remote(1 - core)[:2]:
@@ -212,7 +228,18 @@
             for side in range(2):
                 block = slots[i, side].reshape(8, BLOCK, WIDE).astype(F32)
                 halves.extend(from_blocks(block))
-            operand = jnp.concatenate(halves, axis=1).astype(BF16)
+            squared = halves[0] * halves[0]
+            for half in halves[1:]:
+                squared += half * half
+            column = jnp.sum(squared, axis=1, keepdims=True).reshape(4, OWN, 1)
+            shape = (4, OWN, 128)
+            diagonal = lax.broadcasted_iota(jnp.int32, shape, 1) == lax.broadcasted_iota(jnp.int32, shape, 2)
+            row = jnp.sum(jnp.where(diagonal, column, 0.0), axis=1, keepdims=True)
+            sq_sent[i] = jnp.broadcast_to(row, (4, 8, 128))
+            for copy in cp_sq(i):
+                copy.start()
+            gained = [halves[k] * gain[k // 2, :, pl.ds(k % 2 * WIDE, WIDE)] for k in range(4)]
+            operand = jnp.concatenate(gained, axis=1).astype(BF16)
             for h in range(2):
                 for n in range(HALF // WIDE):
                     columns = pl.ds(h * HALF + n * WIDE, WIDE)
@@ -233,10 +260,13 @@
             to_left.start()
 
         def activate(i):
-            for copy in cp_f(i):
+            for copy in (*cp_f(i), *cp_sq(i)):
                 copy.wait_recv()
+            total = sq_sent[i, y] + sq_got[i, 0] + sq_got[i, 1] + sq_got[i, 2]
+            scale = lax.rsqrt(to_column(total[0:1, :], OWN) / D + 1e-05)
             gate = part[i, y, 0].astype(F32) + rb[i, 0, 0].astype(F32) + rb[i, 1, 0].astype(F32)
             up = part[i, y, 1].astype(F32) + rb[i, 0, 1].astype(F32) + rb[i, 1, 1].astype(F32)
+            gate, up = gate * scale, up * scale
             value = (gate / (1.0 + jnp.exp(-gate)) * up).astype(BF16)
             hid[i, y, 0] = value[:, : HALF // 2]
             hid[i, y, 1] = value[:, HALF // 2 :]
@@ -305,38 +335,42 @@
             cp_d(i, core).start()
 
         def to_group(i):
-            @pl.when(i > 0)
-            def _():
-                cp_a(i).wait_recv()
-
             for j in range(1, 8):
                 cp_c(i, j).start()
 
+        for at, arrived, leaving in ((1, (1, 7), (2, 3)), (2, (2, 3), (4, 5)), (4, (4, 5), (6,)), (6, (6,), ())):
+
+            @pl.when(t == at)
+            def _(arrived=arrived, leaving=leaving):
+                for i in arrived:
+                    cp_a(i).wait_recv()
+                for i in leaving:
+                    cp_a(i).start()
+
+        stage(0, to_group, 1)
         stage(2, gate_up)
         stage(3, second_hop)
+        stage(1, to_twin)
         stage(4, activate)
         stage(5, pass_on)
         stage(6, down)
         stage(7, over_slices)
-        stage(8, give_back)
-        stage(1, to_twin)
-        stage(0, to_group)
+        stage(9, give_back)
         return carry
 
-    lax.fori_loop(0, CHUNKS + 8, step, 0)
+    lax.fori_loop(0, CHUNKS + 9, step, 0)
 
     for i in range(1, CHUNKS):
         cp_l_from(i).wait_recv()
     halves = [half.astype(BF16) for half in from_blocks(ret[...].astype(F32))]
+    over_slots = (((0,), (0,)), ((), ()))
     for h in range(2):
-        got_first = jnp.dot(table_first.astype(BF16), halves[h], preferred_element_type=F32)
-        got_second = jnp.dot(table_second.astype(BF16), halves[h], preferred_element_type=F32)
-        mixed = weight[:, 0:1] * got_first + weight[:, 1:2] * got_second
+        got_first = lax.dot_general(table_first.astype(BF16), halves[h], over_slots, preferred_element_type=F32)
+        got_second = lax.dot_general(table_second.astype(BF16), halves[h], over_slots, preferred_element_type=F32)
+        mixed = weight_of(0) * got_first + weight_of(1) * got_second
         out[:, pl.ds(h * WIDE, WIDE)] = mixed.astype(BF16)
 
-    for j in range(1, 8):
-        cp_sq(j).wait_send()
-    for copy in w_remote(core):
+    for copy in (cp_gain(core), *w_remote(core)):
         copy.wait_send()
 
     def finish(i, carry):
@@ -350,7 +384,7 @@
             cp_j(i, j).wait_send()
         cp_d(i, core).wait_send()
         cp_i(i).wait_send()
-        for copy in (*cp_e(i), *cp_f(i), *cp_g(i, y, y), *cp_h(i, left, right)):
+        for copy in (*cp_sq(i), *cp_e(i), *cp_f(i), *cp_g(i, y, y), *cp_h(i, left, right)):
             copy.wait_send()
         return carry
 
@@ -365,10 +399,17 @@
     result = pl.pallas_call(
         kernel,
         out_shape=jax.ShapeDtypeStruct((LEN, FEAT), BF16),
-        in_specs=[pl.BlockSpec(memory_space=pltpu.SMEM), vmem, vmem, vmem, vmem, whole, whole, whole],
+        in_specs=[pl.BlockSpec(memory_space=pltpu.SMEM)] + [whole] * 7,
         out_specs=vmem,
         scratch_shapes=[
-            pltpu.VMEM((8, LEN, 128), F32),
+            pltpu.VMEM((LEN, FEAT), BF16),
+            pltpu.VMEM((2, 1, FEAT), F32),
+            dma, dma,
+            pltpu.VMEM((2, LEN), jnp.int32),
+            pltpu.VMEM((2, LEN), F32),
+            dma((4,)),
+            pltpu.VMEM((n, 4, 8, 128), F32),
+            pltpu.VMEM((n, 3, 8, 128), F32),
             pltpu.VMEM((EXPERTS, BLOCK, WIDE), BF16),
             pltpu.VMEM((n, 2, 4, 2, BLOCK, WIDE), BF16),
             pltpu.VMEM((2, FEAT, 2 * HALF), BF16),
@@ -384,7 +425,7 @@
             pltpu.VMEM((n, 7, BLOCK, WIDE), BF16),
             pltpu.VMEM((n, BLOCK, WIDE), BF16),
             pltpu.VMEM((EXPERTS, BLOCK, WIDE), BF16),
-            dma((7,)), dma((7,)),
+            dma((n, 3)), dma((n, 3)),
             dma((3,)), dma((3,)), dma((3,)),
             dma((n,)), dma((n,)),
             dma((n, 7)), dma((n, 7)),
@@ -398,10 +439,10 @@
             dma((n,)), dma((n,)),
         ],
         compiler_params=pltpu.CompilerParams(
-            collective_id=0, has_side_effects=True, vmem_limit_bytes=52 << 20
+            collective_id=0, has_side_effects=True, vmem_limit_bytes=60 << 20
         ),
         cost_estimate=pl.CostEstimate(flops=8_000_000_000, bytes_accessed=5_000_000, transcendentals=1_000_000),
-    )(lengths, resid[0], norm_gain[None], route_ids[0], route_weight[0], w_gate, w_up, w_down)
+    )(lengths, resid[0], norm_gain[None], route_ids[0].T, route_weight[0].T, w_gate, w_up, w_down)
     return result[None]
 
 

time: 127 us -> 114 us (0.90)
  the two profiles are of different devices: /device:TPU:6 before, /device:TPU:32 now
where the time goes in v2:
time: 114 us
  Pallas kernels  113 us (99%)
  local copies, waits for them, and re-layouts  1.47 us (1%)
    pallas_call x1, Pallas kernels, on_device(): pl.pallas_call(kernel, out_shape=jax.ShapeDtypeStruct((LEN, FEAT), BF16),...  113 us

profile of v2, /device:TPU:32, one launch (start us, length us, event | category | flops | bytes accessed | tf_op | source)
XLA Modules:
  0.0 114.2 jit_solution(14189821906236717331)
XLA Ops:
  0.0 112.7 %shard_map.82 = bf16[64,512]{1,0:T(8,128)(2,1)} custom-call(s32[64]{0:T(128)} %lengths.1, bf16[64,512]{1,0:T(8,128)(2,1)} %bitcast.10, f32[1,512]{1,0:T(1,128)} %bitcast.11, s32[2,64]{1,0:T(2,128)} %bitcast.12, f32[2,64]{1,0:T(2,128)} %bitcast.13, bf16[512,1536]{1,0:T(8,128)(2,1)} %w_gate.1, bf16[512,1536]{1,0:T(8,128)(2,1)} %w_up.1, bf16[1536,512]{1,0:T(8,128)(2,1)} %w_down.1), custom_call_target="tpu_custom_call" | custom-call | flops 8000000000 | bytes 5000000 | tf_op jit(solution)/shard_map/pallas_call | solution.py:399
  112.7 1.5 %copy.10 = bf16[1,64,512]{2,1,0:T(8,128)(2,1)} copy(bf16[1,64,512]{2,1,0:T(8,128)(2,1)} %bitcast.9) | data formatting | bytes 131072

commit v3 on v2

--- a/solution.py
+++ b/solution.py
@@ -38,7 +38,7 @@
 
 
 def kernel(lengths, resid_in, gain_in, chosen_in, weight_in, w_gate, w_up, w_down, out,
-           resid, gain, gain_s, gain_r, chosen, weight, in_l, sq_sent, sq_got, sent, slots, w_in, w_out, part, ra, rb, hid, out_mine, out_sent, out_got,
+           resid, gain, gain_s, gain_r, chosen, weight, tables, shares, in_l, sq_sent, sq_got, sent, slots, w_in, w_out, part, ra, rb, hid, out_mine, out_sent, out_got,
            xs, xr, ret_sent, ret,
            sq_s, sq_r, w_l, w_s, w_r, a_s, a_r, c_s, c_r, d_s, d_r, e_s, e_r, f_s, f_r, g_s, g_r,
            h_s, h_r, i_s, i_r, j_s, j_r, l_s, l_r):
@@ -179,17 +179,15 @@
     rank = jnp.dot(hits.astype(BF16), before.astype(BF16), preferred_element_type=F32)
     places = lax.broadcasted_iota(jnp.int32, (ROWS, LEN), 0).astype(F32)
 
-    def table(pick):
+    def wide(row):
+        return jnp.concatenate([row, jnp.zeros((1, 128 - LEN), F32)], axis=1)
+
+    def place_for(pick):
         slot = jnp.sum(jnp.where(experts == pick, rank, 0.0), axis=0, keepdims=True)
-        place = jnp.where(live, pick.astype(F32) * CAP + slot, -1.0)
-        return jnp.where(places == place, 1.0, 0.0)
-
-    table_first, table_second = table(first), table(second)
-    choose = (table_first + table_second).astype(BF16)
-
-    def weight_of(k):
-        row = jnp.concatenate([weight[k : k + 1, :], jnp.zeros((1, 128 - LEN), F32)], axis=1)
-        return to_column(row, LEN)
+        return jnp.where(live, pick.astype(F32) * CAP + slot, -1.0)
+
+    chosen_places = (place_for(first), place_for(second))
+    choose = sum(jnp.where(places == place, 1.0, 0.0) for place in chosen_places).astype(BF16)
 
     small[1].wait()
     packed = jnp.dot(choose, resid[...], preferred_element_type=F32)
@@ -206,6 +204,11 @@
     for copy in small[2:]:
         copy.wait()
 
+    lanes = lax.broadcasted_iota(jnp.int32, (LEN, ROWS), 1).astype(F32)
+    for k in range(2):
+        tables[k] = jnp.where(lanes == to_column(wide(chosen_places[k]), LEN), 1.0, 0.0).astype(BF16)
+        shares[k] = jnp.broadcast_to(to_column(wide(weight[k : k + 1, :]), LEN), (LEN, WIDE))
+
     def step(t, carry):
         def stage(offset, body, begin=0):
             i = t - offset
@@ -228,6 +231,15 @@
             for side in range(2):
                 block = slots[i, side].reshape(8, BLOCK, WIDE).astype(F32)
                 halves.extend(from_blocks(block))
+            gained = [halves[k] * gain[k // 2, :, pl.ds(k % 2 * WIDE, WIDE)] for k in range(4)]
+            operand = jnp.concatenate(gained, axis=1).astype(BF16)
+            for h in range(2):
+                for n in range(HALF // WIDE):
+                    columns = pl.ds(h * HALF + n * WIDE, WIDE)
+                    product = jnp.dot(operand[:, :FEAT], w_in[0, :, columns], preferred_element_type=F32)
+                    product += jnp.dot(operand[:, FEAT:], w_in[1, :, columns], preferred_element_type=F32)
+                    part[i, :, h, :, pl.ds(n * WIDE, WIDE)] = product.reshape(4, OWN, WIDE).astype(BF16)
+                cp_e(i)[h].start()
             squared = halves[0] * halves[0]
             for half in halves[1:]:
                 squared += half * half
@@ -237,16 +249,6 @@
             row = jnp.sum(jnp.where(diagonal, column, 0.0), axis=1, keepdims=True)
             sq_sent[i] = jnp.broadcast_to(row, (4, 8, 128))
             for copy in cp_sq(i):
-                copy.start()
-            gained = [halves[k] * gain[k // 2, :, pl.ds(k % 2 * WIDE, WIDE)] for k in range(4)]
-            operand = jnp.concatenate(gained, axis=1).astype(BF16)
-            for h in range(2):
-                for n in range(HALF // WIDE):
-                    columns = pl.ds(h * HALF + n * WIDE, WIDE)
-                    product = jnp.dot(operand[:, :FEAT], w_in[0, :, columns], preferred_element_type=F32)
-                    product += jnp.dot(operand[:, FEAT:], w_in[1, :, columns], preferred_element_type=F32)
-                    part[i, :, h, :, pl.ds(n * WIDE, WIDE)] = product.reshape(4, OWN, WIDE).astype(BF16)
-            for copy in cp_e(i):
                 copy.start()
 
         def second_hop(i):
@@ -327,6 +329,24 @@
             def _():
                 cp_l(i).start()
 
+        def finish(i):
+            @pl.when(i == 0)
+            def _():
+                for copy in (cp_gain(core), *w_remote(core)):
+                    copy.wait_send()
+
+            @pl.when(i > 0)
+            def _():
+                cp_a(i).wait_send()
+
+            for j in range(1, 8):
+                cp_c(i, j).wait_send()
+                cp_j(i, j).wait_send()
+            cp_d(i, core).wait_send()
+            cp_i(i).wait_send()
+            for copy in (*cp_sq(i), *cp_e(i), *cp_f(i), *cp_g(i, y, y), *cp_h(i, left, right)):
+                copy.wait_send()
+
         def to_twin(i):
             for j in range(1, 8):
                 other = (member + 8 - j) % 8
@@ -338,6 +358,10 @@
             for j in range(1, 8):
                 cp_c(i, j).start()
 
+        stage(3, second_hop)
+        stage(2, gate_up)
+        stage(1, to_twin)
+        stage(4, activate)
         for at, arrived, leaving in ((1, (1, 7), (2, 3)), (2, (2, 3), (4, 5)), (4, (4, 5), (6,)), (6, (6,), ())):
 
             @pl.when(t == at)
@@ -348,14 +372,11 @@
                     cp_a(i).start()
 
         stage(0, to_group, 1)
-        stage(2, gate_up)
-        stage(3, second_hop)
-        stage(1, to_twin)
-        stage(4, activate)
         stage(5, pass_on)
         stage(6, down)
         stage(7, over_slices)
         stage(9, give_back)
+        stage(9, finish)
         return carry
 
     lax.fori_loop(0, CHUNKS + 9, step, 0)
@@ -363,32 +384,12 @@
     for i in range(1, CHUNKS):
         cp_l_from(i).wait_recv()
     halves = [half.astype(BF16) for half in from_blocks(ret[...].astype(F32))]
-    over_slots = (((0,), (0,)), ((), ()))
     for h in range(2):
-        got_first = lax.dot_general(table_first.astype(BF16), halves[h], over_slots, preferred_element_type=F32)
-        got_second = lax.dot_general(table_second.astype(BF16), halves[h], over_slots, preferred_element_type=F32)
-        mixed = weight_of(0) * got_first + weight_of(1) * got_second
-        out[:, pl.ds(h * WIDE, WIDE)] = mixed.astype(BF16)
-
-    for copy in (cp_gain(core), *w_remote(core)):
-        copy.wait_send()
-
-    def finish(i, carry):
-        @pl.when(i > 0)
-        def _():
-            cp_a(i).wait_send()
-            cp_l(i).wait_send()
-
-        for j in range(1, 8):
-            cp_c(i, j).wait_send()
-            cp_j(i, j).wait_send()
-        cp_d(i, core).wait_send()
-        cp_i(i).wait_send()
-        for copy in (*cp_sq(i), *cp_e(i), *cp_f(i), *cp_g(i, y, y), *cp_h(i, left, right)):
-            copy.wait_send()
-        return carry
-
-    lax.fori_loop(0, CHUNKS, finish, 0)
+        got = [jnp.dot(tables[k], halves[h], preferred_element_type=F32) for k in range(2)]
+        out[:, pl.ds(h * WIDE, WIDE)] = (shares[0] * got[0] + shares[1] * got[1]).astype(BF16)
+
+    for i in range(1, CHUNKS):
+        cp_l(i).wait_send()
 
 
 def on_device(resid, norm_gain, lengths, route_ids, route_weight, w_gate, w_up, w_down):
@@ -407,6 +408,8 @@
             dma, dma,
             pltpu.VMEM((2, LEN), jnp.int32),
             pltpu.VMEM((2, LEN), F32),
+            pltpu.VMEM((2, LEN, ROWS), BF16),
+            pltpu.VMEM((2, LEN, WIDE), F32),
             dma((4,)),
             pltpu.VMEM((n, 4, 8, 128), F32),
             pltpu.VMEM((n, 3, 8, 128), F32),

time: 114 us -> 111 us (0.974)
  the two profiles are of different devices: /device:TPU:32 before, /device:TPU:6 now
where the time goes in v3:
time: 111 us
  Pallas kernels  110 us (99%)
  local copies, waits for them, and re-layouts  1.47 us (1%)
    pallas_call x1, Pallas kernels, on_device(): pl.pallas_call(kernel, out_shape=jax.ShapeDtypeStruct((LEN, FEAT), BF16),...  110 us

profile of v3, /device:TPU:6, one launch (start us, length us, event | category | flops | bytes accessed | tf_op | source)
XLA Modules:
  0.0 111.1 jit_solution(10645559085652723507)
XLA Ops:
  0.0 109.7 %shard_map.82 = bf16[64,512]{1,0:T(8,128)(2,1)} custom-call(s32[64]{0:T(128)} %lengths.1, bf16[64,512]{1,0:T(8,128)(2,1)} %bitcast.10, f32[1,512]{1,0:T(1,128)} %bitcast.11, s32[2,64]{1,0:T(2,128)} %bitcast.12, f32[2,64]{1,0:T(2,128)} %bitcast.13, bf16[512,1536]{1,0:T(8,128)(2,1)} %w_gate.1, bf16[512,1536]{1,0:T(8,128)(2,1)} %w_up.1, bf16[1536,512]{1,0:T(8,128)(2,1)} %w_down.1), custom_call_target="tpu_custom_call" | custom-call | flops 8000000000 | bytes 5000000 | tf_op jit(solution)/shard_map/pallas_call | solution.py:400
  109.7 1.5 %copy.10 = bf16[1,64,512]{2,1,0:T(8,128)(2,1)} copy(bf16[1,64,512]{2,1,0:T(8,128)(2,1)} %bitcast.9) | data formatting | bytes 131072

commit v4 on v3

--- a/solution.py
+++ b/solution.py
@@ -199,7 +199,7 @@
     cp_a(1).start()
     cp_a(7).start()
     cp_gain(core).start()
-    for copy in w_remote(core):
+    for copy in w_remote(core)[:2]:
         copy.start()
     for copy in small[2:]:
         copy.wait()
@@ -210,10 +210,10 @@
         shares[k] = jnp.broadcast_to(to_column(wide(weight[k : k + 1, :]), LEN), (LEN, WIDE))
 
     def step(t, carry):
-        def stage(offset, body, begin=0):
+        def stage(offset, body, begin=0, end=CHUNKS):
             i = t - offset
 
-            @pl.when((i >= begin) & (i < CHUNKS))
+            @pl.when((i >= begin) & (i < end))
             def _():
                 body(i)
 
@@ -221,10 +221,8 @@
             @pl.when(i == 0)
             def _():
                 cp_gain(1 - core).wait_recv()
-                for copy in w_local()[:2]:
-                    copy.wait()
-                for copy in w_remote(1 - core)[:2]:
-                    copy.wait_recv()
+                w_local()[0].wait()
+                w_remote(1 - core)[0].wait_recv()
 
             cp_d(i, 1 - core).wait_recv()
             halves = []
@@ -234,6 +232,14 @@
             gained = [halves[k] * gain[k // 2, :, pl.ds(k % 2 * WIDE, WIDE)] for k in range(4)]
             operand = jnp.concatenate(gained, axis=1).astype(BF16)
             for h in range(2):
+                if h == 1:
+
+                    @pl.when(i == 0)
+                    def _():
+                        w_local()[1].wait()
+                        w_remote(1 - core)[1].wait_recv()
+                        w_remote(core)[2].start()
+
                 for n in range(HALF // WIDE):
                     columns = pl.ds(h * HALF + n * WIDE, WIDE)
                     product = jnp.dot(operand[:, :FEAT], w_in[0, :, columns], preferred_element_type=F32)
@@ -362,7 +368,7 @@
         stage(2, gate_up)
         stage(1, to_twin)
         stage(4, activate)
-        for at, arrived, leaving in ((1, (1, 7), (2, 3)), (2, (2, 3), (4, 5)), (4, (4, 5), (6,)), (6, (6,), ())):
+        for at, arrived, leaving in ((1, (1, 7), (2, 3)), (2, (2, 3), (4, 5)), (3, (4, 5), (6,)), (5, (6,), ())):
 
             @pl.when(t == at)
             def _(arrived=arrived, leaving=leaving):
@@ -371,15 +377,16 @@
                 for i in leaving:
                     cp_a(i).start()
 
-        stage(0, to_group, 1)
+        stage(0, to_group, 1, 3)
+        stage(-1, to_group, 3)
         stage(5, pass_on)
         stage(6, down)
         stage(7, over_slices)
-        stage(9, give_back)
-        stage(9, finish)
+        stage(8, give_back)
+        stage(8, finish)
         return carry
 
-    lax.fori_loop(0, CHUNKS + 9, step, 0)
+    lax.fori_loop(0, CHUNKS + 8, step, 0)
 
     for i in range(1, CHUNKS):
         cp_l_from(i).wait_recv()

time: 111 us -> 111 us (level); the launches traced: 111 us -> 110 us
    pallas_call x1, Pallas kernels: 110 us -> 109 us  [on_device(): pl.pallas_call(kernel, out_shape=jax.ShapeDtypeStruct((LEN, FEAT), BF16),...]
where the time goes in v4:
time: 111 us; the launch traced here: 110 us
  Pallas kernels  109 us (98%)
  local copies, waits for them, and re-layouts  1.47 us (1%)
    pallas_call x1, Pallas kernels, on_device(): pl.pallas_call(kernel, out_shape=jax.ShapeDtypeStruct((LEN, FEAT), BF16),...  109 us

profile of v4, /device:TPU:6, one launch (start us, length us, event | category | flops | bytes accessed | tf_op | source)
XLA Modules:
  0.0 110.0 jit_solution(13764179408100379634)
XLA Ops:
  0.0 108.5 %shard_map.82 = bf16[64,512]{1,0:T(8,128)(2,1)} custom-call(s32[64]{0:T(128)} %lengths.1, bf16[64,512]{1,0:T(8,128)(2,1)} %bitcast.10, f32[1,512]{1,0:T(1,128)} %bitcast.11, s32[2,64]{1,0:T(2,128)} %bitcast.12, f32[2,64]{1,0:T(2,128)} %bitcast.13, bf16[512,1536]{1,0:T(8,128)(2,1)} %w_gate.1, bf16[512,1536]{1,0:T(8,128)(2,1)} %w_up.1, bf16[1536,512]{1,0:T(8,128)(2,1)} %w_down.1), custom_call_target="tpu_custom_call" | custom-call | flops 8000000000 | bytes 5000000 | tf_op jit(solution)/shard_map/pallas_call | solution.py:407
  108.5 1.5 %copy.10 = bf16[1,64,512]{2,1,0:T(8,128)(2,1)} copy(bf16[1,64,512]{2,1,0:T(8,128)(2,1)} %bitcast.9) | data formatting | bytes 131072
